TPU v7x, 256 devices: a whole 4x4x8 slice. The times are simulated.
256 devices in a mesh: list: 64 (over z_lo, y, x, core), row: 4 (over z_hi).
Axes of the slice: x: 4, y: 4, z: 8 (z_hi: 4, z_lo: 2; z = z_hi * 2 + z_lo), core: 2. Of those that a mesh axis runs over, the one named last changes fastest.
Arguments:
- corpus: bfloat16 [262144, 768], P(('list', 'row')), may hold values from -6 to 6
- row_list: int32 [262144], P(('list', 'row')), may hold values from 0 to 4095, as said below
- list_slot: int32 [4096], replicated, may hold values from 0 to 4095, as said below
- member_counts: int32 [4096], P('list'), may hold values from 32 to 96, as said below
- old_centroids: float32 [4096, 768], P('list'), may hold values from -6 to 6
- next_rows: bfloat16 [393216, 768], P(('list', 'row')), may hold values from -6 to 6
Outputs:
- new_centroids: float32 [4096, 768], P('list')
- best_score: float32 [393216], P(('list', 'row'))
Inputs may be any that keep to these rules, and one draw needn't show every extreme that they name: `row_list`: each device sends every owner (list_slot // 64) at least 8 and at most 24 of its rows; some owner receives 24 rows from every device. `list_slot`: A permutation of the list numbers. `member_counts`: the exact number of corpus rows in each slot's list; the lists of one owner differ by at most one.
All inputs are finite; a program needn't handle non-finite values.
Results may differ from a plain program's by a relative error of at most 0.0025.
Values may be sent and summed in bfloat16 or wider, within the bound.
A program may use at most 64 MiB of HBM per device.

v0:
```python
import jax
import jax.numpy as jnp
from jax import lax
from jax.sharding import PartitionSpec as P

ITERS = 3
eps_norm = 1e-06
aniso_par = 32.0
perp_weight = 1.0
prior_weight = 16.0


def unit_of(row_block):
    values = row_block.astype(jnp.float32)
    scaled = values / jnp.sqrt(jnp.sum(values * values, axis=1, keepdims=True) + eps_norm)
    return scaled.astype(jnp.bfloat16)


def split_pair(values):
    high_part = values.astype(jnp.bfloat16)
    low_part = (values - high_part.astype(jnp.float32)).astype(jnp.bfloat16)
    return (high_part, low_part)


def prepare(member_block, member_local, lists_own):
    unit_rows = unit_of(member_block)
    membership = (member_local[:, None] == jnp.arange(lists_own, dtype=jnp.int32)[None, :]).astype(
        jnp.float32
    )
    return (unit_rows, membership)


def gram_part(unit_rows, membership, vectors):
    inner_dims = (((1,), (1,)), ((), ()))
    outer_dims = (((0,), (0,)), ((), ()))
    vec_high, vec_low = split_pair(vectors)
    scores = lax.dot_general(unit_rows, vec_high, inner_dims, preferred_element_type=jnp.float32)
    scores = scores + lax.dot_general(
        unit_rows, vec_low, inner_dims, preferred_element_type=jnp.float32
    )
    weighted = scores * membership
    wgt_high, wgt_low = split_pair(weighted)
    result = lax.dot_general(wgt_high, unit_rows, outer_dims, preferred_element_type=jnp.float32)
    return result + lax.dot_general(
        wgt_low, unit_rows, outer_dims, preferred_element_type=jnp.float32
    )


def member_total(membership, member_block):
    return lax.dot_general(
        membership.astype(jnp.bfloat16),
        member_block,
        (((0,), (0,)), ((), ())),
        preferred_element_type=jnp.float32,
    )


def on_device(corpus, row_list, list_slot, member_counts, old_centroids, next_rows):
    n_owner = lax.axis_size("list")
    lists_own = old_centroids.shape[0]
    local_rows = corpus.shape[0]
    cap_slots = 3 * local_rows // (2 * n_owner)
    width = corpus.shape[1]
    slot_ids = jnp.take(list_slot, row_list)
    owner_id = slot_ids // lists_own
    local_id = slot_ids % lists_own
    hits = (owner_id[:, None] == jnp.arange(n_owner, dtype=jnp.int32)[None, :]).astype(jnp.int32)
    rank_in = jnp.sum((jnp.cumsum(hits, axis=0) - 1) * hits, axis=1)
    dest_idx = owner_id * cap_slots + rank_in
    send_rows = (
        jnp.zeros((n_owner * cap_slots, width), jnp.bfloat16)
        .at[dest_idx]
        .set(corpus)
        .reshape(n_owner, cap_slots, width)
    )
    send_local = (
        jnp.full((n_owner * cap_slots,), -1, jnp.int32)
        .at[dest_idx]
        .set(local_id)
        .reshape(n_owner, cap_slots)
    )
    recv_rows, recv_local = (
        lax.all_to_all(send_rows, "list", split_axis=0, concat_axis=0, tiled=True),
        lax.all_to_all(send_local, "list", split_axis=0, concat_axis=0, tiled=True),
    )
    recv_rows = recv_rows.reshape(n_owner * cap_slots, width)
    recv_local = recv_local.reshape(n_owner * cap_slots)
    centroids = old_centroids
    unit_rows, membership = prepare(recv_rows, recv_local, lists_own)
    row_sums, first_gram = lax.psum(
        (member_total(membership, recv_rows), gram_part(unit_rows, membership, centroids)), "row"
    )
    diag_term = perp_weight * member_counts.astype(jnp.float32)[:, None] + prior_weight
    residual = (
        aniso_par * row_sums
        + prior_weight * centroids
        - (diag_term * centroids + (aniso_par - perp_weight) * first_gram)
    )
    direction = residual
    norm_now = jnp.sum(residual * residual, axis=1, keepdims=True)
    for iteration in range(ITERS):
        applied = diag_term * direction + (aniso_par - perp_weight) * lax.psum(
            gram_part(unit_rows, membership, direction), "row"
        )
        step_len = norm_now / jnp.sum(direction * applied, axis=1, keepdims=True)
        centroids = centroids + step_len * direction
        residual = residual - step_len * applied
        norm_next = jnp.sum(residual * residual, axis=1, keepdims=True)
        direction = residual + norm_next / norm_now * direction
        norm_now = norm_next
    panel = centroids.astype(jnp.bfloat16)
    start_score = jnp.full((next_rows.shape[0],), -jnp.inf, jnp.float32)
    piece = lax.all_gather(panel, "list", axis=0, tiled=True)
    piece_rows = piece.shape[0]
    block_size = 512
    blocks = piece.reshape(piece_rows // block_size, block_size, piece.shape[1])

    def one_block(running, piece_block):
        scores = lax.dot_general(
            next_rows, piece_block, (((1,), (1,)), ((), ())), preferred_element_type=jnp.float32
        )
        return (jnp.maximum(running, jnp.max(scores, axis=1)), None)

    result, unused = lax.scan(one_block, start_score, blocks)
    return (centroids, result / width)


def solution(mesh):
    in_specs = (
        P(("list", "row"), None),
        P(("list", "row")),
        P(),
        P("list"),
        P("list", None),
        P(("list", "row"), None),
    )
    out_specs = (P("list", None), P(("list", "row")))
    return jax.shard_map(
        on_device, mesh=mesh, in_specs=in_specs, out_specs=out_specs, check_vma=False
    )
```

profile of v0, /device:TPU:1, one launch (start us, length us, event | category | flops | bytes accessed | tf_op | source)
XLA Modules:
  0.0 470.4 jit_solution(17790374509922220616)
XLA Ops:
  7.2 0.8 fusion.41
  7.9 6.1 %gather_fusion = s32[1024]{0:T(1024)S(1)} fusion(s32[4096]{0:T(1024)S(1)} %copy-done, s32[1024]{0:T(1024)S(1)} %fusion.41), kind=kCustom, calls=%fused_computation | custom fusion | bytes 12288 | tf_op jit(solution)/shard_map/jit(_take)/gather | solution.py:64
  14.2 18.0 %reduce-window.6 = s32[64,8,128]{2,1,0:T(8,128)S(1)} reduce-window(s32[64,8,128]{2,1,0:T(8,128)S(1)} %fusion.11, s32[]{:T(128)} %constant.69.clone.1), window={size=1x1x128 pad=0_0x0_0x127_0}, to_apply=%region_0.1 | reduce-window | flops 8323072 | bytes 524292 | tf_op jit(solution)/shard_map/reduce-window
  32.2 0.1 slice.10
  32.3 0.1 copy.10
  32.5 0.1 copy.11
  32.6 0.1 add_add_fusion
  32.7 0.1 fusion.10
  32.8 4.3 scatter_custom_fusion
  37.1 0.7 all_to_all.9
  37.8 10.3 %all-to-all-start = ((s32[64,1,24]{2,1,0:T(1,128)}), s32[64,1,24]{2,1,0:T(1,128)S(1)}, u32[]{:S(2)}, u32[]{:S(2)}) async-start(s32[64,1,24]{2,1,0:T(1,128)} %bitcast.3), calls=%async_computation | async-start | bytes 65536 | tf_op jit(solution)/shard_map/all_to_all | solution.py:84
  48.2 7.5 %scatter_custom_fusion.1 = bf16[1536,768]{1,0:T(8,128)(2,1)} fusion(s32[1024]{0:T(1024)S(1)} %compare_select_fusion, bf16[1024,768]{1,0:T(8,128)(2,1)} %param.8, bf16[]{:T(256)} %constant.79.clone.1), kind=kCustom, calls=%fused_computation.18 | custom fusion | bytes 2359808 | tf_op jit(solution)/shard_map/scatter | solution.py:73
  55.7 0.3 all-to-all-done
  55.9 8.6 %all-to-all-start.1 = ((bf16[64,24,768]{2,1,0:T(8,128)(2,1)}), bf16[64,24,768]{2,1,0:T(8,128)(2,1)S(1)}, u32[]{:S(2)}, u32[]{:S(2)}) async-start(bf16[64,24,768]{2,1,0:T(8,128)(2,1)} %bitcast.46), calls=%async_computation.1 | async-start | bytes 4718592 | tf_op jit(solution)/shard_map/all_to_all | solution.py:83
  64.6 0.5 broadcast.126
  65.1 0.7 reduce.5
  65.9 0.1 eq.47
  65.9 29.0 %all-to-all-done.1 = bf16[64,24,768]{2,1,0:T(8,128)(2,1)S(1)} async-done(((bf16[64,24,768]{2,1,0:T(8,128)(2,1)}), bf16[64,24,768]{2,1,0:T(8,128)(2,1)S(1)}, u32[]{:S(2)}, u32[]{:S(2)}) %all-to-all-start.1) | async-done | bytes 2359328 | tf_op jit(solution)/shard_map/all_to_all | solution.py:83
  95.0 0.5 multiply_reduce_fusion
  95.5 0.9 copy-done.1
  96.4 0.1 sqrt.12
  96.5 2.2 divide_convert_fusion
  98.7 0.8 fusion.36
  99.5 0.8 fusion.6
  100.4 0.5 fusion.24
  100.9 1.2 convolution_add_fusion.7
  102.1 1.2 fusion.12
  103.3 0.2 all-reduce.6.cloned.1.call-start
  103.6 52.9 %all-reduce.12.cloned.1.call-done = (f32[64,768]{1,0:T(8,128)}, f32[64,768]{1,0:T(8,128)}) async-done(((f32[64,768]{1,0:T(8,128)}, f32[64,768]{1,0:T(8,128)}), (f32[64,768]{1,0:T(8,128)}, f32[64,768]{1,0:T(8,128)})) %all-reduce.12.cloned.1.call-update) | async-done | bytes 393232 | tf_op jit(solution)/shard_map/psum | solution.py:90
  156.4 1.1 add_subtract_fusion
  157.6 0.8 fusion.33
  158.4 0.8 fusion.5
  159.2 0.5 fusion.21
  159.7 1.2 convolution_add_fusion.6
  161.0 49.5 %all-reduce.6.cloned.1.call-done = f32[64,768]{1,0:T(8,128)} async-done(((f32[64,768]{1,0:T(8,128)}), f32[64,768]{1,0:T(8,128)}) %all-reduce.6.cloned.1.call-update) | async-done | bytes 196624 | tf_op jit(solution)/shard_map/psum | solution.py:102
  210.5 1.1 multiply_reduce_fusion.5
  211.7 1.1 multiply_reduce_fusion.4
  212.8 0.1 multiply_add_fusion.3
  212.9 0.8 fusion.30
  213.8 0.8 fusion.4
  214.6 0.5 fusion.18
  215.1 1.2 convolution_add_fusion.5
  216.4 49.2 %all-reduce.8.cloned.1.call-done = f32[64,768]{1,0:T(8,128)} async-done(((f32[64,768]{1,0:T(8,128)}), f32[64,768]{1,0:T(8,128)}) %all-reduce.8.cloned.1.call-update) | async-done | bytes 196624 | tf_op jit(solution)/shard_map/psum | solution.py:102
  265.6 1.1 multiply_reduce_fusion.3
  266.8 1.1 multiply_reduce_fusion.2
  267.9 1.1 multiply_add_fusion.1
  269.0 0.8 fusion.27
  269.8 0.8 fusion.3
  270.7 0.5 fusion.15
  271.2 1.2 convolution_add_fusion.4
  272.5 49.3 %all-reduce.10.cloned.1.call-done = f32[64,768]{1,0:T(8,128)} async-done(((f32[64,768]{1,0:T(8,128)}), f32[64,768]{1,0:T(8,128)}) %all-reduce.10.cloned.1.call-update) | async-done | bytes 196624 | tf_op jit(solution)/shard_map/psum | solution.py:102
  321.8 1.1 multiply_reduce_fusion.1
  322.9 0.8 fusion.43
  323.7 112.5 %all-gather.2.cloned.1.call-done = bf16[4096,768]{1,0:T(8,128)(2,1)} async-done(((bf16[64,768]{1,0:T(8,128)(2,1)}), bf16[4096,768]{1,0:T(8,128)(2,1)}) %all-gather.2.cloned.1.call-update) | async-done | bytes 6291472 | tf_op jit(solution)/shard_map/all_gather | solution.py:113
  436.2 27.1 %while.11 = (s32[]{:T(128)}, f32[1536]{0:T(1024)S(1)}, bf16[8,512,768]{2,1,0:T(8,128)(2,1)}, bf16[1536,768]{1,0:T(8,128)(2,1)}, s32[]{:T(128)}, /*index=5*/s32[]{:T(128)}) while((s32[]{:T(128)}, f32[1536]{0:T(1024)S(1)}, bf16[8,512,768]{2,1,0:T(8,128)(2,1)}, bf16[1536,768]{1,0:T(8,128)(2,1)}, s32[]{:T(128)}, ...), condition=%wide.region_19.20_spmd.clone, body=%wide.region_17.19_spmd.clone.sunk | while | flops 1208747520 | bytes 3170895 | solution.py:124
  436.2 3.3 convolution_reduce_fusion.2
  439.6 3.3 convolution_reduce_fusion.2
  443.0 3.3 convolution_reduce_fusion.2
  446.4 3.3 convolution_reduce_fusion.2
  449.8 3.3 convolution_reduce_fusion.2
  453.2 3.3 convolution_reduce_fusion.2
  456.5 3.3 convolution_reduce_fusion.2
  459.9 3.3 convolution_reduce_fusion.2
  463.3 0.6 broadcast_multiply_fusion
  (41 shorter events, 0.5 us)
Async XLA Ops:
  7.2 0.8 copy-start
  7.2 6.9 %copy-start.4 = (s32[1024]{0:T(1024)S(1)}, s32[1024]{0:T(1024)}, u32[]{:S(2)}) copy-start(s32[1024]{0:T(1024)} %param.9) | copy-start | bytes 12292
  37.8 18.1 %all-to-all-start = ((s32[64,1,24]{2,1,0:T(1,128)}), s32[64,1,24]{2,1,0:T(1,128)S(1)}, u32[]{:S(2)}, u32[]{:S(2)}) async-start(s32[64,1,24]{2,1,0:T(1,128)} %bitcast.3), calls=%async_computation | async-start | bytes 65536 | tf_op jit(solution)/shard_map/all_to_all | solution.py:84
  55.9 39.0 %all-to-all-start.1 = ((bf16[64,24,768]{2,1,0:T(8,128)(2,1)}), bf16[64,24,768]{2,1,0:T(8,128)(2,1)S(1)}, u32[]{:S(2)}, u32[]{:S(2)}) async-start(bf16[64,24,768]{2,1,0:T(8,128)(2,1)} %bitcast.46), calls=%async_computation.1 | async-start | bytes 4718592 | tf_op jit(solution)/shard_map/all_to_all | solution.py:83
  64.6 91.9 %all-reduce.12.cloned.1.call-start = ((), (), s32[]{:S(2)}) async-start(), calls=%async_computation.6 | async-start | bytes 786432 | tf_op jit(solution)/shard_map/psum | solution.py:90
  95.0 1.4 copy-start.1
  96.5 2.2 copy-start.3
  100.4 1.7 copy-start.2
  100.9 2.7 copy-start.5
  103.3 107.2 %all-reduce.6.cloned.1.call-start = ((), (), s32[]{:S(2)}) async-start(), calls=%async_computation.2 | async-start | bytes 393216 | tf_op jit(solution)/shard_map/psum | solution.py:102
  161.0 104.7 %all-reduce.8.cloned.1.call-start = ((), (), s32[]{:S(2)}) async-start(), calls=%async_computation.3 | async-start | bytes 393216 | tf_op jit(solution)/shard_map/psum | solution.py:102
  216.3 105.4 %all-reduce.10.cloned.1.call-start = ((), (), s32[]{:S(2)}) async-start(), calls=%async_computation.4 | async-start | bytes 393216 | tf_op jit(solution)/shard_map/psum | solution.py:102
  272.4 163.8 %all-gather.2.cloned.1.call-start = ((), (), s32[]{:S(2)}) async-start(), calls=%async_computation.5 | async-start | bytes 6389760 | tf_op jit(solution)/shard_map/all_gather | solution.py:113
Sparse Core Ops, SparseCore 0:
  103.5 52.9 all-reduce.11
  161.1 49.3 all-reduce.5
  216.5 49.1 all-reduce.7
  272.5 49.1 all-reduce.9
  323.9 112.3 all-gather.1
where the time goes:
time: 471 us; the launch traced here: 470 us
  waiting for transfers between devices  343 us (73%)
  matrix products  41.5 us (9%)
  other arithmetic  31.9 us (7%)
  local copies, waits for them, and re-layouts  20.6 us (4%)
  starting transfers between devices  19.3 us (4%)
  between operations  14.1 us (3%)
    psum x3, waiting for transfers between devices, on_device(): lax.psum(gram_part(unit_rows, membership, direction), 'row')  148 us
    all_gather x1, waiting for transfers between devices, on_device(): piece = lax.all_gather(panel, 'list', axis=0, tiled=True)  112 us
    psum x1, waiting for transfers between devices, on_device(): lax.psum((member_total(membership, recv_rows), gram_part(unit_rows, membe...  52.9 us
    all_to_all x1, waiting for transfers between devices, on_device(): lax.all_to_all(send_rows, 'list', split_axis=0, concat_axis=0, tiled=True)  29 us
    dot_general x8, matrix products, one_block(): lax.dot_general(next_rows, piece_block, (((1,), (1,)), ((), ())), preferr...  26.8 us
    another operation x2, other arithmetic  18 us
    all_to_all x1, starting transfers between devices, on_device(): lax.all_to_all(send_local, 'list', split_axis=0, concat_axis=0, tiled=True)  10.3 us
  transfers between devices with their start and end apart: 7, of which 7 were waited for; matrix products, arithmetic and copies ran while one was open for 2% of the time, Pallas kernels for 0%

commit v1 on v0

--- a/solution.py
+++ b/solution.py
@@ -110,7 +110,13 @@
         norm_now = norm_next
     panel = centroids.astype(jnp.bfloat16)
     start_score = jnp.full((next_rows.shape[0],), -jnp.inf, jnp.float32)
-    piece = lax.all_gather(panel, "list", axis=0, tiled=True)
+    trace_windows = lambda sheet, comm_axis: jnp.concatenate(
+        jax.lax.all_to_all(
+            jnp.stack([sheet] * jax.lax.axis_size(comm_axis), axis=0), comm_axis, 0, 0
+        ),
+        0,
+    )
+    piece = trace_windows(panel, "list")
     piece_rows = piece.shape[0]
     block_size = 512
     blocks = piece.reshape(piece_rows // block_size, block_size, piece.shape[1])

time: 471 us -> 451 us (0.958); the launches traced: 470 us -> 442 us
  waiting for transfers between devices: 343 us -> 307 us
  starting transfers between devices: 19.3 us -> 29.7 us
  matrix products: 41.5 us -> 35.2 us
    all_gather x1 -> x0, waiting for transfers between devices: 112 us -> none  [on_device(): piece = lax.all_gather(panel, 'list', axis=0, tiled=True)]
    all_to_all x0 -> x1, waiting for transfers between devices: none -> 76.9 us  [on_device(): jax.lax.all_to_all(jnp.stack([sheet] * jax.lax.axis_size(comm_axis), axis...]
    all_to_all x0 -> x1, starting transfers between devices: none -> 10.4 us  [on_device(): jax.lax.all_to_all(jnp.stack([sheet] * jax.lax.axis_size(comm_axis), axis...]
    dot_general x8, matrix products: 26.8 us -> 20.5 us  [one_block(): lax.dot_general(next_rows, piece_block, (((1,), (1,)), ((), ())), preferr...]
where the time goes in v1:
time: 451 us; the launch traced here: 442 us
  waiting for transfers between devices  307 us (68%)
  matrix products  35.2 us (8%)
  other arithmetic  31.9 us (7%)
  starting transfers between devices  29.7 us (7%)
  local copies, waits for them, and re-layouts  24 us (5%)
  between operations  14.1 us (3%)
    psum x3, waiting for transfers between devices, on_device(): lax.psum(gram_part(unit_rows, membership, direction), 'row')  148 us
    all_to_all x1, waiting for transfers between devices, on_device(): jax.lax.all_to_all(jnp.stack([sheet] * jax.lax.axis_size(comm_axis), axis...  76.9 us
    psum x1, waiting for transfers between devices, on_device(): lax.psum((member_total(membership, recv_rows), gram_part(unit_rows, membe...  52.9 us
    all_to_all x1, waiting for transfers between devices, on_device(): lax.all_to_all(send_rows, 'list', split_axis=0, concat_axis=0, tiled=True)  29 us
    dot_general x8, matrix products, one_block(): lax.dot_general(next_rows, piece_block, (((1,), (1,)), ((), ())), preferr...  20.5 us
    another operation x2, other arithmetic  18 us
    all_to_all x1, starting transfers between devices, on_device(): jax.lax.all_to_all(jnp.stack([sheet] * jax.lax.axis_size(comm_axis), axis...  10.4 us
    all_to_all x1, starting transfers between devices, on_device(): lax.all_to_all(send_local, 'list', split_axis=0, concat_axis=0, tiled=True)  10.3 us
  transfers between devices with their start and end apart: 7, of which 7 were waited for; matrix products, arithmetic and copies ran while one was open for 2% of the time, Pallas kernels for 0%

profile of v1, /device:TPU:1, one launch (start us, length us, event | category | flops | bytes accessed | tf_op | source)
XLA Modules:
  0.0 442.3 jit_solution(16413994300570559885)
XLA Ops:
  7.2 0.8 fusion.41
  7.9 6.1 %gather_fusion = s32[1024]{0:T(1024)S(1)} fusion(s32[4096]{0:T(1024)S(1)} %copy-done, s32[1024]{0:T(1024)S(1)} %fusion.41), kind=kCustom, calls=%fused_computation | custom fusion | bytes 12288 | tf_op jit(solution)/shard_map/jit(_take)/gather | solution.py:64
  14.2 18.0 %reduce-window.6 = s32[64,8,128]{2,1,0:T(8,128)S(1)} reduce-window(s32[64,8,128]{2,1,0:T(8,128)S(1)} %fusion.11, s32[]{:T(128)} %constant.69.clone.1), window={size=1x1x128 pad=0_0x0_0x127_0}, to_apply=%region_0.1 | reduce-window | flops 8323072 | bytes 524292 | tf_op jit(solution)/shard_map/reduce-window
  32.2 0.1 slice.10
  32.3 0.1 copy.10
  32.5 0.1 copy.11
  32.6 0.1 add_add_fusion
  32.8 4.3 scatter_custom_fusion
  37.1 0.7 all_to_all.12
  37.8 10.3 %all-to-all-start = ((s32[64,1,24]{2,1,0:T(1,128)}), s32[64,1,24]{2,1,0:T(1,128)S(1)}, u32[]{:S(2)}, u32[]{:S(2)}) async-start(s32[64,1,24]{2,1,0:T(1,128)} %bitcast.3), calls=%async_computation | async-start | bytes 65536 | tf_op jit(solution)/shard_map/all_to_all | solution.py:84
  48.2 7.5 %scatter_custom_fusion.1 = bf16[1536,768]{1,0:T(8,128)(2,1)} fusion(s32[1024]{0:T(1024)S(1)} %compare_select_fusion, bf16[1024,768]{1,0:T(8,128)(2,1)} %param.8, bf16[]{:T(256)} %constant.79.clone.1), kind=kCustom, calls=%fused_computation.18 | custom fusion | bytes 2359808 | tf_op jit(solution)/shard_map/scatter | solution.py:73
  55.7 0.3 all-to-all-done
  55.9 8.6 %all-to-all-start.1 = ((bf16[64,24,768]{2,1,0:T(8,128)(2,1)}), bf16[64,24,768]{2,1,0:T(8,128)(2,1)S(1)}, u32[]{:S(2)}, u32[]{:S(2)}) async-start(bf16[64,24,768]{2,1,0:T(8,128)(2,1)} %bitcast.46), calls=%async_computation.1 | async-start | bytes 4718592 | tf_op jit(solution)/shard_map/all_to_all | solution.py:83
  64.6 0.5 broadcast.128
  65.1 0.7 reduce.5
  65.9 0.1 eq.47
  65.9 29.0 %all-to-all-done.1 = bf16[64,24,768]{2,1,0:T(8,128)(2,1)S(1)} async-done(((bf16[64,24,768]{2,1,0:T(8,128)(2,1)}), bf16[64,24,768]{2,1,0:T(8,128)(2,1)S(1)}, u32[]{:S(2)}, u32[]{:S(2)}) %all-to-all-start.1) | async-done | bytes 2359328 | tf_op jit(solution)/shard_map/all_to_all | solution.py:83
  95.0 0.5 multiply_reduce_fusion
  95.5 0.9 copy-done.1
  96.5 2.2 divide_convert_fusion
  98.7 0.8 fusion.36
  99.5 0.8 fusion.6
  100.4 0.5 fusion.24
  100.9 1.2 convolution_add_fusion.7
  102.1 1.2 fusion.12
  103.3 0.2 all-reduce.6.cloned.1.call-start
  103.6 52.9 %all-reduce.12.cloned.1.call-done = (f32[64,768]{1,0:T(8,128)}, f32[64,768]{1,0:T(8,128)}) async-done(((f32[64,768]{1,0:T(8,128)}, f32[64,768]{1,0:T(8,128)}), (f32[64,768]{1,0:T(8,128)}, f32[64,768]{1,0:T(8,128)})) %all-reduce.12.cloned.1.call-update) | async-done | bytes 393232 | tf_op jit(solution)/shard_map/psum | solution.py:90
  156.4 1.1 add_subtract_fusion
  157.6 0.8 fusion.33
  158.4 0.8 fusion.5
  159.2 0.5 fusion.21
  159.7 1.2 convolution_add_fusion.6
  161.0 49.5 %all-reduce.6.cloned.1.call-done = f32[64,768]{1,0:T(8,128)} async-done(((f32[64,768]{1,0:T(8,128)}), f32[64,768]{1,0:T(8,128)}) %all-reduce.6.cloned.1.call-update) | async-done | bytes 196624 | tf_op jit(solution)/shard_map/psum | solution.py:102
  210.5 1.1 multiply_reduce_fusion.5
  211.7 1.1 multiply_reduce_fusion.4
  212.8 0.1 multiply_add_fusion.3
  212.9 0.8 fusion.30
  213.8 0.8 fusion.4
  214.6 0.5 fusion.18
  215.1 1.2 convolution_add_fusion.5
  216.4 49.2 %all-reduce.8.cloned.1.call-done = f32[64,768]{1,0:T(8,128)} async-done(((f32[64,768]{1,0:T(8,128)}), f32[64,768]{1,0:T(8,128)}) %all-reduce.8.cloned.1.call-update) | async-done | bytes 196624 | tf_op jit(solution)/shard_map/psum | solution.py:102
  265.6 1.1 multiply_reduce_fusion.3
  266.8 1.1 multiply_reduce_fusion.2
  267.9 1.1 multiply_add_fusion.1
  269.0 0.8 fusion.27
  269.8 0.8 fusion.3
  270.7 0.5 fusion.15
  271.2 1.2 convolution_add_fusion.4
  272.4 49.3 %all-reduce.10.cloned.1.call-done = f32[64,768]{1,0:T(8,128)} async-done(((f32[64,768]{1,0:T(8,128)}), f32[64,768]{1,0:T(8,128)}) %all-reduce.10.cloned.1.call-update) | async-done | bytes 196624 | tf_op jit(solution)/shard_map/psum | solution.py:102
  321.8 1.1 multiply_reduce_fusion.1
  322.9 0.8 fusion.43
  323.7 3.4 stack.2
  327.1 10.4 %all-to-all-start.2 = ((bf16[64,64,768]{2,1,0:T(8,128)(2,1)}), bf16[64,64,768]{2,1,0:T(8,128)(2,1)}, u32[]{:S(2)}, u32[]{:S(2)}) async-start(bf16[64,64,768]{2,1,0:T(8,128)(2,1)} %stack.2), calls=%async_computation.2 | async-start | bytes 12582912 | tf_op jit(solution)/shard_map/all_to_all | solution.py:114
  337.5 76.9 %all-to-all-done.2 = bf16[64,64,768]{2,1,0:T(8,128)(2,1)} async-done(((bf16[64,64,768]{2,1,0:T(8,128)(2,1)}), bf16[64,64,768]{2,1,0:T(8,128)(2,1)}, u32[]{:S(2)}, u32[]{:S(2)}) %all-to-all-start.2) | async-done | bytes 6291488 | tf_op jit(solution)/shard_map/all_to_all | solution.py:114
  414.4 20.8 %while.11 = (s32[]{:T(128)}, f32[1536]{0:T(1024)S(1)}, bf16[8,512,768]{2,1,0:T(8,128)(2,1)}, bf16[1536,768]{1,0:T(8,128)(2,1)S(1)}, s32[]{:T(128)}, /*index=5*/s32[]{:T(128)}) while((s32[]{:T(128)}, f32[1536]{0:T(1024)S(1)}, bf16[8,512,768]{2,1,0:T(8,128)(2,1)}, bf16[1536,768]{1,0:T(8,128)(2,1)S(1)}, s32[]{:T(128)}, ...), condition=%wide.region_19.20_spmd.clone, body=%wide.region_17.19_spmd.clone.sunk | while | flops 1208747520 | bytes 3170895 | solution.py:130
  414.4 2.6 convolution_reduce_fusion.2
  417.0 2.6 convolution_reduce_fusion.2
  419.6 2.6 convolution_reduce_fusion.2
  422.2 2.6 convolution_reduce_fusion.2
  424.8 2.6 convolution_reduce_fusion.2
  427.4 2.6 convolution_reduce_fusion.2
  430.0 2.6 convolution_reduce_fusion.2
  432.6 2.6 convolution_reduce_fusion.2
  435.2 0.6 broadcast_multiply_fusion
  (43 shorter events, 0.5 us)
Async XLA Ops:
  7.2 0.8 copy-start
  7.2 6.9 %copy-start.4 = (s32[1024]{0:T(1024)S(1)}, s32[1024]{0:T(1024)}, u32[]{:S(2)}) copy-start(s32[1024]{0:T(1024)} %param.9) | copy-start | bytes 12292
  37.8 18.1 %all-to-all-start = ((s32[64,1,24]{2,1,0:T(1,128)}), s32[64,1,24]{2,1,0:T(1,128)S(1)}, u32[]{:S(2)}, u32[]{:S(2)}) async-start(s32[64,1,24]{2,1,0:T(1,128)} %bitcast.3), calls=%async_computation | async-start | bytes 65536 | tf_op jit(solution)/shard_map/all_to_all | solution.py:84
  55.9 39.0 %all-to-all-start.1 = ((bf16[64,24,768]{2,1,0:T(8,128)(2,1)}), bf16[64,24,768]{2,1,0:T(8,128)(2,1)S(1)}, u32[]{:S(2)}, u32[]{:S(2)}) async-start(bf16[64,24,768]{2,1,0:T(8,128)(2,1)} %bitcast.46), calls=%async_computation.1 | async-start | bytes 4718592 | tf_op jit(solution)/shard_map/all_to_all | solution.py:83
  64.6 91.9 %all-reduce.12.cloned.1.call-start = ((), (), s32[]{:S(2)}) async-start(), calls=%async_computation.6 | async-start | bytes 786432 | tf_op jit(solution)/shard_map/psum | solution.py:90
  95.0 1.4 copy-start.1
  96.5 2.2 copy-start.3
  100.4 1.7 copy-start.2
  100.9 2.7 copy-start.6
  103.3 107.2 %all-reduce.6.cloned.1.call-start = ((), (), s32[]{:S(2)}) async-start(), calls=%async_computation.3 | async-start | bytes 393216 | tf_op jit(solution)/shard_map/psum | solution.py:102
  161.0 104.7 %all-reduce.8.cloned.1.call-start = ((), (), s32[]{:S(2)}) async-start(), calls=%async_computation.4 | async-start | bytes 393216 | tf_op jit(solution)/shard_map/psum | solution.py:102
  216.3 105.4 %all-reduce.10.cloned.1.call-start = ((), (), s32[]{:S(2)}) async-start(), calls=%async_computation.5 | async-start | bytes 393216 | tf_op jit(solution)/shard_map/psum | solution.py:102
  327.1 87.3 %copy-start.5 = (bf16[1536,768]{1,0:T(8,128)(2,1)S(1)}, bf16[1536,768]{1,0:T(8,128)(2,1)}, u32[]{:S(2)}) copy-start(bf16[1536,768]{1,0:T(8,128)(2,1)} %param.13) | copy-start | bytes 7077892
  327.1 87.3 %all-to-all-start.2 = ((bf16[64,64,768]{2,1,0:T(8,128)(2,1)}), bf16[64,64,768]{2,1,0:T(8,128)(2,1)}, u32[]{:S(2)}, u32[]{:S(2)}) async-start(bf16[64,64,768]{2,1,0:T(8,128)(2,1)} %stack.2), calls=%async_computation.2 | async-start | bytes 12582912 | tf_op jit(solution)/shard_map/all_to_all | solution.py:114
Sparse Core Ops, SparseCore 0:
  103.5 52.9 all-reduce.11
  161.1 49.3 all-reduce.5
  216.5 49.1 all-reduce.7
  272.5 49.1 all-reduce.9
